TPU v7x, 32 devices: a whole 2x2x4 slice. The times are simulated.
32 devices in a mesh: groups: 2 (over x), tensor: 16 (over z, y, core).
Axes of the slice: x: 2, y: 2, z: 4, core: 2. Of those that a mesh axis runs over, the one named last changes fastest.
Arguments:
- attention_output_rows: bfloat16 [512, 8192], P(('groups', 'tensor')), parts along dimension 0, may hold values from -6 to 6
- output_projection_weight: bfloat16 [8192, 8192], P(None, 'tensor'), may hold values from -0.0625 to 0.0625
- adapter_down_matrices: bfloat16 [256, 8192, 64], P(None, 'tensor'), may hold values from -0.0625 to 0.0625
- adapter_up_matrices: bfloat16 [256, 64, 8192], P(None, None, 'tensor'), may hold values from -0.75 to 0.75
- picks: int32 [512, 2], P('groups'), parts along dimension 0, may hold values from 0 to 255, all different within a row; in each aligned block of 256 rows (0 to 255, 256 to 511, ...) at most 8 rows name the same one
- gates: float32 [512, 2], P('groups'), parts along dimension 0, may hold values from 0.2 to 1
- adapter_storage_index: int32 [256], replicated, may hold values from 0 to 255, each once
Outputs:
- mixed: bfloat16 [512, 8192], P('groups', 'tensor'), parts along dimension 0
There are 2 independent parts, one for each index of `groups`. A program takes and returns all parts, laid end to end along the dimension named above; an argument that names none is the same for every part. Nothing has to cross between parts.
Inputs may be any that keep to these rules, and one draw needn't show every extreme that they name: `picks`: each token names two different adapters; over the 256 tokens of a replica no adapter is named more than 8 times, a bound that some block reaches. A permutation: the matrices of adapter e lie at index adapter_storage_index[e] of adapter_down_matrices and adapter_up_matrices.
All inputs are finite; a program needn't handle non-finite values.
Results may differ from a plain program's by a relative error of at most 0.0038.
Values may be sent and summed in bfloat16 or wider, within the bound.
A program may use at most 128 MiB of HBM per device.

v0:
```python
import jax
import jax.numpy as jnp
from jax import lax
from jax.sharding import PartitionSpec as P


def routing(picks, gates, adapter_storage_index, storage_count, most):
    chosen = picks.reshape(-1)
    slot_of = jnp.take(adapter_storage_index, chosen)
    onehot = (slot_of[:, None] == jnp.arange(storage_count, dtype=jnp.int32)[None, :]).astype(
        jnp.int32
    )
    order_in = jnp.sum((jnp.cumsum(onehot, axis=0) - onehot) * onehot, axis=1)
    position = slot_of * most + order_in
    token_ids = jnp.arange(chosen.shape[0], dtype=jnp.int32) // 2
    token_of = jnp.zeros((storage_count * most,), jnp.int32).at[position].set(token_ids)
    token_gate_weight = (
        jnp.zeros((storage_count * most,), jnp.float32).at[position].set(gates.reshape(-1))
    )
    live = (
        jnp.zeros((storage_count * most,), jnp.float32)
        .at[position]
        .set(jnp.ones_like(gates.reshape(-1)))
    )
    return (token_of, token_gate_weight, live)


def on_device(
    attention_output_rows,
    output_projection_weight,
    adapter_down_matrices,
    adapter_up_matrices,
    picks,
    gates,
    adapter_storage_index,
):
    storage_count = adapter_down_matrices.shape[0]
    most = max(2, 8 * picks.shape[0] // storage_count)
    columns = output_projection_weight.shape[1]
    gathered = lax.all_gather(attention_output_rows, "tensor", axis=0, tiled=True)
    base = jnp.dot(gathered, output_projection_weight, preferred_element_type=jnp.float32)
    own_block = lax.dynamic_slice_in_dim(gathered, lax.axis_index("tensor") * columns, columns, 1)
    token_of, token_gate_weight, live = routing(
        picks, gates, adapter_storage_index, storage_count, most
    )
    routed_token_rows = (own_block[token_of] * live[:, None].astype(own_block.dtype)).reshape(
        storage_count, most, columns
    )
    local_partial_output = jnp.einsum(
        "kit,ktn->kin", routed_token_rows, adapter_down_matrices, preferred_element_type=jnp.float32
    )
    reduced_rank_rows = lax.psum(local_partial_output, "tensor").astype(jnp.bfloat16)
    expanded_rows = jnp.einsum(
        "hou,hut->hot", reduced_rank_rows, adapter_up_matrices, preferred_element_type=jnp.float32
    )
    expanded_rows = expanded_rows * token_gate_weight.reshape(storage_count, most)[:, :, None]
    total = base.at[token_of].add(expanded_rows.reshape(storage_count * most, columns))
    return total.astype(jnp.bfloat16)


def solution(mesh):
    placed = (
        P(("groups", "tensor"), None),
        P(None, "tensor"),
        P(None, "tensor", None),
        P(None, None, "tensor"),
        P("groups", None),
        P("groups", None),
        P(),
    )
    return jax.shard_map(
        on_device, mesh=mesh, in_specs=placed, out_specs=P("groups", "tensor"), check_vma=False
    )
```

profile of v0, /device:TPU:0, one launch (start us, length us, event | category | flops | bytes accessed | tf_op | source)
XLA Modules:
  0.0 188.0 jit_solution(1515289318981301391)
XLA Ops:
  6.5 0.0 copy-start
  6.5 0.0 all-gather.2.cloned.1.call-start
  6.5 0.7 all-gather.2.cloned.1.call-update
  7.3 0.8 copy.8
  8.1 0.1 reshape.131
  8.2 0.1 reshape.133
  8.4 0.1 reshape.132
  8.5 0.0 copy-done
  8.6 3.5 %gather_fusion = s32[512]{0:T(512)S(1)} fusion(s32[256]{0:T(256)S(1)} %copy-done, s32[1024]{0:T(1024)S(1)} %pad_clamp_fusion), kind=kCustom, calls=%fused_computation | custom fusion | bytes 6144 | tf_op jit(solution)/shard_map/jit(_take)/gather | solution.py:9
  12.1 0.1 copy.11
  12.2 0.8 copy.13
  13.0 0.1 reshape.173
  13.2 0.2 fusion.10
  13.5 0.1 copy.12
  13.6 0.2 fusion.7
  13.9 2.5 %scatter_custom_fusion.2 = f32[2048]{0:T(1024)S(1)} fusion(s32[512]{0:T(512)S(1)} %bitcast.39, f32[512]{0:T(512)S(1)} %reshape.173, f32[]{:T(128)} %constant.53.clone.1), kind=kCustom, calls=%fused_computation.33 | custom fusion | bytes 8196 | tf_op jit(solution)/shard_map/scatter | solution.py:18
  16.3 2.5 %scatter_custom_fusion.1 = f32[2048]{0:T(1024)S(1)} fusion(s32[512]{0:T(512)S(1)} %bitcast.40, f32[512]{0:T(512)S(1)} %broadcast.136, f32[]{:T(128)} %constant.53.clone.1), kind=kCustom, calls=%fused_computation.35 | custom fusion | bytes 8196 | tf_op jit(solution)/shard_map/scatter | solution.py:23
  18.8 2.5 %scatter_custom_fusion = s32[2048]{0:T(1024)S(1)} fusion(s32[512]{0:T(512)S(1)} %bitcast.41, s32[512]{0:T(512)S(1)} %add_select_fusion, s32[]{:T(128)} %constant.27.clone.1), kind=kCustom, calls=%fused_computation.40 | custom fusion | bytes 8196 | tf_op jit(solution)/shard_map/scatter | solution.py:16
  21.3 0.7 mul.44
  22.0 0.1 mul.47
  22.1 40.7 %all-gather.2.cloned.1.call-done = bf16[256,8192]{1,0:T(8,128)(2,1)} async-done(((bf16[16,8192]{1,0:T(8,128)(2,1)}), bf16[256,8192]{1,0:T(8,128)(2,1)}) %all-gather.2.cloned.1.call-update) | async-done | bytes 4194320 | tf_op jit(solution)/shard_map/all_gather | solution.py:40
  62.8 1.0 constant_dynamic-slice_fusion
  63.8 7.5 %gather_fusion.1 = bf16[2048,512]{1,0:T(8,128)(2,1)S(1)} fusion(bf16[256,512]{1,0:T(8,128)(2,1)S(1)} %constant_dynamic-slice_fusion, s32[2048]{0:T(1024)S(1)} %get-tuple-element.5), kind=kCustom, calls=%fused_computation.1 | custom fusion | bytes 4202496 | tf_op jit(solution)/shard_map/gather | solution.py:46
  71.3 8.1 %fusion.3 = f32[256,8,64]{2,1,0:T(8,128)S(1)} fusion(bf16[256,512,64]{1,2,0:T(8,128)(2,1)} %param.9, bf16[2048,512]{1,0:T(8,128)(2,1)S(1)} %gather_fusion.1, bf16[256,8]{1,0:T(8,128)(2,1)} %mul.44), kind=kOutput, calls=%fused_computation.10 | convolution fusion | flops 135266304 | bytes 19402752 | tf_op jit(solution)/shard_map/kit,ktn->kin/dot_general | solution.py:49
  79.5 71.0 %all-reduce.1 = bf16[256,8,64]{2,1,0:T(8,128)(2,1)S(1)} all-reduce(f32[256,8,64]{2,1,0:T(8,128)S(1)} %fusion.3), channel_id=1, replica_groups=mesh['groups'=2,'tensor'=16] {'tensor'}, use_global_device_ids=true, to_apply=%region_5.6 | all-reduce | flops 131072 | bytes 786432 | tf_op jit(solution)/shard_map/psum | solution.py:52
  150.5 0.0 copy-start.1
  150.5 10.2 %fusion.23 = f32[256,8,512]{2,1,0:T(8,128)} fusion(bf16[256,8,64]{2,1,0:T(8,128)(2,1)S(1)} %all-reduce.1, bf16[256,64,512]{2,1,0:T(8,128)(2,1)} %param.10), kind=kOutput, calls=%fused_computation.50 | convolution fusion | flops 134217728 | bytes 21233664 | tf_op jit(solution)/shard_map/hou,hut->hot/dot_general | solution.py:53
  160.7 0.0 copy-done.1
  160.7 5.7 %fusion.22 = f32[256,512]{1,0:T(8,128)S(1)} fusion(bf16[256,8192]{1,0:T(8,128)(2,1)S(1)} %copy-done.1, bf16[8192,512]{1,0:T(8,128)(2,1)} %param.8), kind=kOutput, calls=%fused_computation.49 | convolution fusion | flops 2147483648 | bytes 13107200 | tf_op jit(solution)/shard_map/dot_general | solution.py:41
  166.4 14.0 %scatter_custom_fusion.3 = f32[256,512]{1,0:T(8,128)S(1)} fusion(f32[256,512]{1,0:T(8,128)S(1)} %fusion.22, s32[2048]{0:T(1024)S(1)} %get-tuple-element.6, f32[256,8,512]{2,1,0:T(8,128)} %fusion.23, f32[256,8]{1,0:T(8,128)S(1)} %mul.47), kind=kCustom, calls=%fused_computation.6 | custom fusion | flops 2097152 | bytes 4849664 | tf_op jit(solution)/shard_map/scatter-add | solution.py:57
  180.4 0.7 convert_element_type.21
  (14 shorter events, 0.1 us)
Async XLA Ops:
  6.5 2.0 %copy-start = (s32[256]{0:T(256)S(1)}, s32[256]{0:T(256)}, u32[]{:S(2)}) copy-start(s32[256]{0:T(256)} %param.13) | copy-start | bytes 3076
  6.5 56.3 %all-gather.2.cloned.1.call-start = ((), (), s32[]{:S(2)}) async-start(), calls=%async_computation | async-start | bytes 4456448 | tf_op jit(solution)/shard_map/all_gather | solution.py:40
  150.5 10.2 %copy-start.1 = (bf16[256,8192]{1,0:T(8,128)(2,1)S(1)}, bf16[256,8192]{1,0:T(8,128)(2,1)}, u32[]{:S(2)}) copy-start(bf16[256,8192]{1,0:T(8,128)(2,1)} %all-gather.2.cloned.1.call-done) | copy-start | bytes 12582916
Sparse Core Ops, SparseCore 0:
  9.5 53.2 all-gather.1
where the time goes:
time: 188 us
  blocking collectives  71 us (38%)
  waiting for transfers between devices  41.4 us (22%)
  matrix products  24 us (13%)
  local copies, waits for them, and re-layouts  22.6 us (12%)
  other arithmetic  15.3 us (8%)
  between operations  13.6 us (7%)
    psum x1, blocking collectives, on_device(): lax.psum(local_partial_output, 'tensor').astype(jnp.bfloat16)  71 us
    all_gather x1, waiting for transfers between devices, on_device(): lax.all_gather(attention_output_rows, 'tensor', axis=0, tiled=True)  40.7 us
    scatter-add x1, other arithmetic, on_device(): base.at[token_of].add(expanded_rows.reshape(storage_count * most, columns))  14 us
    dot_general x1, matrix products, on_device(): jnp.einsum('hou,hut->hot', reduced_rank_rows, adapter_up_matrices, prefer...  10.2 us
    dot_general x1, matrix products, on_device(): jnp.einsum('kit,ktn->kin', routed_token_rows, adapter_down_matrices, pref...  8.14 us
    gather x1, local copies, waits for them, and re-layouts, on_device(): own_block[token_of] * live[:, None].astype(own_block.dtype)  7.54 us
    dot_general x1, matrix products, on_device(): jnp.dot(gathered, output_projection_weight, preferred_element_type=jnp.fl...  5.69 us
  transfers between devices with their start and end apart: 1, of which 1 were waited for; matrix products, arithmetic and copies ran while one was open for 8% of the time, Pallas kernels for 0%

commit v1 on v0

v1 whole, which is shorter than its diff:
```python
import functools

import jax
import jax.numpy as jnp
from jax import lax
from jax.experimental import pallas as pl
from jax.experimental.pallas import tpu as pltpu
from jax.sharding import PartitionSpec as P

MESH = pl.DeviceIdType.MESH
Z, Y, C = 4, 2, 2
N = Z * Y * C
Q = 4
LOADS = 16


def fused(
    x_ref, w_ref, down_ref, up_ref, picks_ref, gates_ref, index_ref, out_ref,
    gathered, block, w_vm, down_vm, up_vm, product, mixed_rows, partial, pieces, reduced, total,
    load_sem, w_sem, own_sem, a2a_send, a2a_recv, z_send, y_send, c_send, recv,
    rs_send, rs_recv, ag_send, ag_recv,
):
    rows = x_ref.shape[0]
    tokens = rows * N
    feat = block.shape[1]
    kq = gathered.shape[2]
    stored = index_ref.shape[0]
    rank = down_ref.shape[0] // stored
    per = stored // LOADS
    span = per * rank
    me = lax.axis_index("tensor")
    z = me // (Y * C)
    yc = me % (Y * C)
    y = yc // C
    c = yc % C

    def dev(zz, yy, cc):
        return (zz * Y + yy) * C + cc

    loads = []
    for i in range(LOADS):
        cp = pltpu.make_async_copy(
            down_ref.at[pl.ds(i * span, span)], down_vm.at[pl.ds(i * span, span)], load_sem.at[0, i])
        cp.start()
    own = []
    for q in range(Q):
        cp = pltpu.make_async_copy(
            x_ref.at[:, pl.ds(q * kq, kq)], gathered.at[q, pl.ds(pl.multiple_of(me * rows, rows), rows)], own_sem.at[q])
        cp.start()
        own.append(cp)
    own_block = pltpu.make_async_copy(
        x_ref.at[:, pl.ds(pl.multiple_of(me * feat, feat), feat)],
        block.at[pl.ds(pl.multiple_of(me * rows, rows), rows)], own_sem.at[Q])
    own_block.start()
    for i in range(LOADS):
        pltpu.make_async_copy(
            up_ref.at[pl.ds(i * span, span)], up_vm.at[pl.ds(i * span, span)], load_sem.at[1, i]).start()
    for q in range(Q):
        pltpu.make_async_copy(
            w_ref.at[pl.ds(q * kq, kq)], w_vm.at[pl.ds(q * kq, kq)], w_sem.at[q]).start()

    barrier = pltpu.get_barrier_semaphore()
    for d in range(1, N):
        pl.semaphore_signal(barrier, inc=1, device_id={"tensor": (me + d) % N}, device_id_type=MESH)
    pl.semaphore_wait(barrier, N - 1)

    sends = []

    def send(src, dst, ssem, rsem, target, cond=None):
        cp = pltpu.make_async_remote_copy(
            src_ref=src, dst_ref=dst, send_sem=ssem, recv_sem=rsem,
            device_id={"tensor": target}, device_id_type=MESH)
        if cond is None:
            cp.start()
        else:
            pl.when(cond)(cp.start)
        sends.append((cp, cond))

    for d in range(1, N):
        to = (me + d) % N
        send(x_ref.at[:, pl.ds(pl.multiple_of(to * feat, feat), feat)],
             block.at[pl.ds(pl.multiple_of(me * rows, rows), rows)],
             a2a_send.at[d], a2a_recv.at[d], to)

    def place(q, origin):
        return gathered.at[q, pl.ds(pl.multiple_of(origin * rows, rows), rows)]

    for q in range(Q):
        src = x_ref.at[:, pl.ds(q * kq, kq)]
        dst = place(q, me)
        send(src, dst, z_send.at[0, q], recv.at[q, me], dev(z + 1, y, c), z < Z - 1)
        send(src, dst, z_send.at[1, q], recv.at[q, me], dev(z - 1, y, c), z > 0)
        send(src, dst, y_send.at[0, q], recv.at[q, me], dev(z, 1 - y, c))
        send(src, dst, c_send.at[0, q], recv.at[q, me], dev(z, y, 1 - c))

    far = [None, z + 1 - 2 * (z % 2), 2 - z // 2, 3 - 3 * (z // 2)]
    hop = [None, 3 - z, 3 * (z - 1), 3 * (z - 1)]
    middle = (z == 1) | (z == 2)

    def wait_in(q, origin):
        ref = place(q, origin)
        pltpu.make_async_remote_copy(
            src_ref=ref, dst_ref=ref, send_sem=y_send.at[0, q], recv_sem=recv.at[q, origin],
            device_id={"tensor": dev(z, y, 1 - c)}, device_id_type=MESH).wait_recv()

    def z_event(d, q):
        origin = dev(far[d], y, c)
        wait_in(q, origin)
        ref = place(q, origin)
        send(ref, ref, z_send.at[1 + d, q], recv.at[q, origin], dev(hop[d], y, c), middle)
        send(ref, ref, y_send.at[d, q], recv.at[q, origin], dev(z, 1 - y, c))
        send(ref, ref, c_send.at[d, q], recv.at[q, origin], dev(z, y, 1 - c))

    def y_event(d, q):
        origin = dev(z if d == 0 else far[d], 1 - y, c)
        wait_in(q, origin)
        ref = place(q, origin)
        send(ref, ref, c_send.at[4 + d, q], recv.at[q, origin], dev(z, y, 1 - c))

    picks = picks_ref[...]

    def look(e, slot):
        return jnp.where(picks == e, index_ref[e], slot)

    slot = lax.fori_loop(0, stored, look, jnp.zeros_like(picks), unroll=8)

    own_block.wait()
    for d in range(1, N):
        frm = (me + N - d) % N
        ref = block.at[pl.ds(pl.multiple_of(frm * rows, rows), rows)]
        pltpu.make_async_remote_copy(
            src_ref=ref, dst_ref=ref, send_sem=a2a_send.at[d], recv_sem=a2a_recv.at[d],
            device_id={"tensor": frm}, device_id_type=MESH).wait_recv()

    def load_wait(which, src, vm, i):
        at = pl.ds(pl.multiple_of(i * span, span), span)
        pltpu.make_async_copy(src.at[at], vm.at[at], load_sem.at[which, i]).wait()

    slot0, slot1 = slot[0:1], slot[1:2]

    def shrink(i, carry):
        load_wait(0, down_ref, down_vm, i)
        at = pl.ds(pl.multiple_of(i * span, span), span)
        res = lax.dot_general(down_vm[at, :], block[...], (((1,), (1,)), ((), ())),
                              preferred_element_type=jnp.float32)
        first, second = carry
        s0, s1 = slot0 - i * per, slot1 - i * per
        for e in range(per):
            part = res[e * rank:(e + 1) * rank]
            first = jnp.where(s0 == e, part, first)
            second = jnp.where(s1 == e, part, second)
        return first, second

    zero = jnp.zeros((rank, tokens), jnp.float32)
    carry = lax.fori_loop(0, LOADS // 2, shrink, (zero, zero))
    for q in range(Q):
        z_event(1, q)
    carry = lax.fori_loop(LOADS // 2, LOADS, shrink, carry)
    each = 2 * rank // N
    for k in range(2):
        for j in range(N // 2):
            partial[k * (N // 2) + j] = carry[k][j * each:(j + 1) * each]
    pieces[0] = partial[me]
    for d in range(1, N):
        to = (me + d) % N
        send(partial.at[to], pieces.at[d], rs_send.at[d], rs_recv.at[d], to)
    for q in range(Q):
        y_event(0, q)
    for q in range(Q):
        z_event(2, q)
    for d in range(1, N):
        pltpu.make_async_remote_copy(
            src_ref=pieces.at[d], dst_ref=pieces.at[d], send_sem=rs_send.at[d], recv_sem=rs_recv.at[d],
            device_id={"tensor": (me + N - d) % N}, device_id_type=MESH).wait_recv()
    mine = pieces[0]
    for d in range(1, N):
        mine = mine + pieces[d]
    half = tokens // 2
    reduced[me] = jnp.concatenate([mine[:, :half], mine[:, half:]], axis=0).astype(jnp.bfloat16)
    for d in range(1, N):
        to = (me + d) % N
        send(reduced.at[me], reduced.at[me], ag_send.at[d], ag_recv.at[d], to)
    for q in range(Q):
        y_event(1, q)
    for d in range(1, N):
        frm = (me + N - d) % N
        pltpu.make_async_remote_copy(
            src_ref=reduced.at[frm], dst_ref=reduced.at[frm], send_sem=ag_send.at[d], recv_sem=ag_recv.at[d],
            device_id={"tensor": frm}, device_id_type=MESH).wait_recv()

    gates = gates_ref[...]
    upper = (lax.broadcasted_iota(jnp.int32, (2 * rank, tokens), 0) >= rank).astype(jnp.int32)
    vectors, marks = [], []
    for k in range(2):
        flat = []
        for j in range(N // 2):
            piece = reduced[k * (N // 2) + j].astype(jnp.float32)
            flat.append(jnp.concatenate([piece[:each], piece[each:]], axis=1))
        flat = jnp.concatenate(flat + flat, axis=0) * gates[k:k + 1]
        vectors.append(jnp.transpose(flat).astype(jnp.bfloat16))
        mark = (slot[k:k + 1] - upper).astype(jnp.float32)
        marks.append(jnp.transpose(mark).astype(jnp.bfloat16))

    total[...] = jnp.zeros_like(total)

    def expand(i, _):
        load_wait(1, up_ref, up_vm, i)
        at = pl.ds(pl.multiple_of(i * span, span), span)
        base = (i * per).astype(jnp.float32).astype(jnp.bfloat16)
        m0, m1 = marks[0] - base, marks[1] - base
        nil = jnp.zeros_like(vectors[0])
        for j in range(per // 2):
            v = jnp.where(m0 == 2 * j, vectors[0], jnp.where(m1 == 2 * j, vectors[1], nil))
            mixed_rows[:, j * 2 * rank:(j + 1) * 2 * rank] = v
        total[...] += jnp.dot(mixed_rows[...], up_vm[at, :], preferred_element_type=jnp.float32)
        return 0

    lax.fori_loop(0, LOADS // 2, expand, 0)
    for q in range(Q):
        z_event(3, q)
    for q in range(Q):
        y_event(2, q)
    lax.fori_loop(LOADS // 2, LOADS, expand, 0)
    for q in range(Q):
        y_event(3, q)

    for q in range(Q):
        own[q].wait()
        for zz in [z] + far[1:]:
            for yy in (y, 1 - y):
                wait_in(q, dev(zz, yy, 1 - c))
        pltpu.make_async_copy(
            w_ref.at[pl.ds(q * kq, kq)], w_vm.at[pl.ds(q * kq, kq)], w_sem.at[q]).wait()
        part = total[...] + jnp.dot(
            gathered[q], w_vm[pl.ds(q * kq, kq), :], preferred_element_type=jnp.float32)
        if q < Q - 1:
            total[...] = part
        else:
            out_ref[...] = part.astype(out_ref.dtype)

    for cp, cond in sends:
        if cond is None:
            cp.wait_send()
        else:
            pl.when(cond)(cp.wait_send)


def by_kernel(rows, weight, down, up, picks, gates, index):
    stored, feat, rank = down.shape
    tokens = picks.shape[0]
    width = weight.shape[0]
    columns = weight.shape[1]
    span = stored // LOADS * rank
    any_ = pl.BlockSpec(memory_space=pl.ANY)
    vm = pl.BlockSpec(memory_space=pltpu.VMEM)
    dma = pltpu.SemaphoreType.DMA
    return pl.pallas_call(
        fused,
        out_shape=jax.ShapeDtypeStruct((tokens, columns), jnp.bfloat16),
        in_specs=[any_, any_, any_, any_, vm, vm, pl.BlockSpec(memory_space=pltpu.SMEM)],
        out_specs=vm,
        scratch_shapes=[
            pltpu.VMEM((Q, tokens, width // Q), jnp.bfloat16),
            pltpu.VMEM((tokens, feat), jnp.bfloat16),
            pltpu.VMEM((width, columns), jnp.bfloat16),
            pltpu.VMEM((stored * rank, feat), jnp.bfloat16),
            pltpu.VMEM((stored * rank, columns), jnp.bfloat16),
            pltpu.VMEM((8, 128), jnp.float32),
            pltpu.VMEM((tokens, span), jnp.bfloat16),
            pltpu.VMEM((N, 2 * rank // N, tokens), jnp.float32),
            pltpu.VMEM((N, 2 * rank // N, tokens), jnp.float32),
            pltpu.VMEM((N, 4 * rank // N, tokens // 2), jnp.bfloat16),
            pltpu.VMEM((tokens, columns), jnp.float32),
            dma((2, LOADS)), dma((Q,)), dma((Q + 1,)), dma((N,)), dma((N,)),
            dma((5, Q)), dma((4, Q)), dma((8, Q)), dma((Q, N)),
            dma((N,)), dma((N,)), dma((N,)), dma((N,)),
        ],
        compiler_params=pltpu.CompilerParams(
            collective_id=0, has_side_effects=True, vmem_limit_bytes=60 * 2**20),
        cost_estimate=pl.CostEstimate(
            flops=2 * tokens * columns * (width + 2 * stored * rank),
            bytes_accessed=2 * (weight.size + down.size + up.size), transcendentals=0),
    )(
        rows, weight, jnp.swapaxes(down, 1, 2).reshape(stored * rank, feat),
        up.reshape(stored * rank, columns), picks.T, gates.T, index,
    )


def routing(picks, gates, adapter_storage_index, storage_count, most):
    chosen = picks.reshape(-1)
    slot_of = jnp.take(adapter_storage_index, chosen)
    onehot = (slot_of[:, None] == jnp.arange(storage_count, dtype=jnp.int32)[None, :]).astype(
        jnp.int32
    )
    order_in = jnp.sum((jnp.cumsum(onehot, axis=0) - onehot) * onehot, axis=1)
    position = slot_of * most + order_in
    token_ids = jnp.arange(chosen.shape[0], dtype=jnp.int32) // 2
    token_of = jnp.zeros((storage_count * most,), jnp.int32).at[position].set(token_ids)
    token_gate_weight = (
        jnp.zeros((storage_count * most,), jnp.float32).at[position].set(gates.reshape(-1))
    )
    live = (
        jnp.zeros((storage_count * most,), jnp.float32)
        .at[position]
        .set(jnp.ones_like(gates.reshape(-1)))
    )
    return (token_of, token_gate_weight, live)


def by_collectives(rows, weight, down, up, picks, gates, index):
    storage_count = down.shape[0]
    most = max(2, 8 * picks.shape[0] // storage_count)
    columns = weight.shape[1]
    gathered = lax.all_gather(rows, "tensor", axis=0, tiled=True)
    base = jnp.dot(gathered, weight, preferred_element_type=jnp.float32)
    own_block = lax.dynamic_slice_in_dim(gathered, lax.axis_index("tensor") * columns, columns, 1)
    token_of, token_gate_weight, live = routing(picks, gates, index, storage_count, most)
    routed = (own_block[token_of] * live[:, None].astype(own_block.dtype)).reshape(
        storage_count, most, columns
    )
    partial = jnp.einsum("kit,ktn->kin", routed, down, preferred_element_type=jnp.float32)
    reduced = lax.psum(partial, "tensor").astype(jnp.bfloat16)
    expanded = jnp.einsum("hou,hut->hot", reduced, up, preferred_element_type=jnp.float32)
    expanded = expanded * token_gate_weight.reshape(storage_count, most)[:, :, None]
    total = base.at[token_of].add(expanded.reshape(storage_count * most, columns))
    return total.astype(jnp.bfloat16)


def solution(mesh):
    placed = (
        P(("groups", "tensor"), None),
        P(None, "tensor"),
        P(None, "tensor", None),
        P(None, None, "tensor"),
        P("groups", None),
        P("groups", None),
        P(),
    )
    body = by_kernel if mesh.shape["tensor"] == N else by_collectives
    return jax.shard_map(
        body, mesh=mesh, in_specs=placed, out_specs=P("groups", "tensor"), check_vma=False
    )
```

time: 188 us -> 60.7 us (0.32)
  blocking collectives: 71 us -> 0 us
  Pallas kernels: 0 us -> 58.4 us
  waiting for transfers between devices: 41.4 us -> 0 us
  matrix products: 24 us -> 0 us
  local copies, waits for them, and re-layouts: 22.6 us -> 1.67 us
  other arithmetic: 15.3 us -> 0 us
  between operations: 13.6 us -> 0.01 us
    psum x1 -> x0, blocking collectives: 71 us -> none  [on_device(): lax.psum(local_partial_output, 'tensor').astype(jnp.bfloat16)]
    pallas_call x0 -> x1, Pallas kernels: none -> 58.4 us  [by_kernel(): pl.pallas_call(fused, out_shape=jax.ShapeDtypeStruct((tokens, columns), j...]
    all_gather x1 -> x0, waiting for transfers between devices: 40.7 us -> none  [on_device(): lax.all_gather(attention_output_rows, 'tensor', axis=0, tiled=True)]
    dot_general x3 -> x0, matrix products: 24 us -> none  [the longest x1 10.2 us: on_device(): jnp.einsum('hou,hut->hot', reduced_rank_rows, adapter_up_matrices, prefer...]
    scatter-add x1 -> x0, other arithmetic: 14 us -> none  [on_device(): base.at[token_of].add(expanded_rows.reshape(storage_count * most, columns))]
    gather x2 -> x0, local copies, waits for them, and re-layouts: 11.1 us -> none  [the longest x1 7.54 us: on_device(): own_block[token_of] * live[:, None].astype(own_block.dtype)]
    scatter x3 -> x0, local copies, waits for them, and re-layouts: 7.35 us -> none  [the longest x1 2.45 us: routing(): jnp.zeros((storage_count * most,), jnp.float32).at[position]]
  transfers between devices with their start and end apart: 1 -> 0, of which waited for: 1 -> 0; matrix products, arithmetic and copies ran while one was open for 8% -> 0% of each run, Pallas kernels for 0% -> 0%
where the time goes in v1:
time: 60.7 us; the launch traced here: 60 us
  Pallas kernels  58.4 us (96%)
  local copies, waits for them, and re-layouts  1.67 us (3%)
    pallas_call x1, Pallas kernels, by_kernel(): pl.pallas_call(fused, out_shape=jax.ShapeDtypeStruct((tokens, columns), j...  58.4 us
    unnamed x1, local copies, waits for them, and re-layouts  1.67 us

profile of v1, /device:TPU:0, one launch (start us, length us, event | category | flops | bytes accessed | tf_op | source)
XLA Modules:
  0.0 60.0 jit_solution(8968680309645488134)
XLA Ops:
  0.0 58.4 %shard_map.73 = bf16[256,512]{1,0:T(8,128)(2,1)} custom-call(bf16[16,8192]{1,0:T(8,128)(2,1)} %x_ref.1, bf16[8192,512]{1,0:T(8,128)(2,1)} %w_ref.1, bf16[16384,512]{1,0:T(8,128)(2,1)} %bitcast.6, bf16[16384,512]{1,0:T(8,128)(2,1)} %bitcast.7, s32[2,256]{1,0:T(2,128)} %bitcast.8, f32[2,256]{1,0:T(2,128)} %bitcast.9, s32[256]{0:T(256)} %index_ref.1), custom_call_target="tpu_custom_call" | custom-call | flops 10737418240 | bytes 41943040 | tf_op jit(solution)/shard_map/pallas_call | solution.py:257
  58.4 1.7 %copy.9 = bf16[256,512]{1,0:T(8,128)(2,1)} copy(bf16[256,512]{1,0:T(8,128)(2,1)} %shard_map.73) | data formatting | bytes 524288

commit v2 on v1

--- a/solution.py
+++ b/solution.py
@@ -11,12 +11,12 @@
 Z, Y, C = 4, 2, 2
 N = Z * Y * C
 Q = 4
-LOADS = 16
+LOADS = 8
 
 
 def fused(
     x_ref, w_ref, down_ref, up_ref, picks_ref, gates_ref, index_ref, out_ref,
-    gathered, block, w_vm, down_vm, up_vm, product, mixed_rows, partial, pieces, reduced, total,
+    gathered, block, w_vm, down_vm, up_vm, mixed_rows, partial, pieces, reduced, total,
     load_sem, w_sem, own_sem, a2a_send, a2a_recv, z_send, y_send, c_send, recv,
     rs_send, rs_recv, ag_send, ag_recv,
 ):
@@ -37,11 +37,6 @@
     def dev(zz, yy, cc):
         return (zz * Y + yy) * C + cc
 
-    loads = []
-    for i in range(LOADS):
-        cp = pltpu.make_async_copy(
-            down_ref.at[pl.ds(i * span, span)], down_vm.at[pl.ds(i * span, span)], load_sem.at[0, i])
-        cp.start()
     own = []
     for q in range(Q):
         cp = pltpu.make_async_copy(
@@ -54,10 +49,7 @@
     own_block.start()
     for i in range(LOADS):
         pltpu.make_async_copy(
-            up_ref.at[pl.ds(i * span, span)], up_vm.at[pl.ds(i * span, span)], load_sem.at[1, i]).start()
-    for q in range(Q):
-        pltpu.make_async_copy(
-            w_ref.at[pl.ds(q * kq, kq)], w_vm.at[pl.ds(q * kq, kq)], w_sem.at[q]).start()
+            down_ref.at[pl.ds(i * span, span)], down_vm.at[pl.ds(i * span, span)], load_sem.at[0, i]).start()
 
     barrier = pltpu.get_barrier_semaphore()
     for d in range(1, N):
@@ -141,6 +133,7 @@
     def shrink(i, carry):
         load_wait(0, down_ref, down_vm, i)
         at = pl.ds(pl.multiple_of(i * span, span), span)
+        pltpu.make_async_copy(up_ref.at[at], up_vm.at[at], load_sem.at[1, i]).start()
         res = lax.dot_general(down_vm[at, :], block[...], (((1,), (1,)), ((), ())),
                               preferred_element_type=jnp.float32)
         first, second = carry
@@ -155,7 +148,10 @@
     carry = lax.fori_loop(0, LOADS // 2, shrink, (zero, zero))
     for q in range(Q):
         z_event(1, q)
-    carry = lax.fori_loop(LOADS // 2, LOADS, shrink, carry)
+        carry = lax.fori_loop(LOADS // 2 + q, LOADS // 2 + q + 1, shrink, carry)
+    for q in range(Q):
+        pltpu.make_async_copy(
+            w_ref.at[pl.ds(q * kq, kq)], w_vm.at[pl.ds(q * kq, kq)], w_sem.at[q]).start()
     each = 2 * rank // N
     for k in range(2):
         for j in range(N // 2):
@@ -182,6 +178,7 @@
         send(reduced.at[me], reduced.at[me], ag_send.at[d], ag_recv.at[d], to)
     for q in range(Q):
         y_event(1, q)
+        z_event(3, q)
     for d in range(1, N):
         frm = (me + N - d) % N
         pltpu.make_async_remote_copy(
@@ -216,8 +213,6 @@
         return 0
 
     lax.fori_loop(0, LOADS // 2, expand, 0)
-    for q in range(Q):
-        z_event(3, q)
     for q in range(Q):
         y_event(2, q)
     lax.fori_loop(LOADS // 2, LOADS, expand, 0)
@@ -265,7 +260,6 @@
             pltpu.VMEM((width, columns), jnp.bfloat16),
             pltpu.VMEM((stored * rank, feat), jnp.bfloat16),
             pltpu.VMEM((stored * rank, columns), jnp.bfloat16),
-            pltpu.VMEM((8, 128), jnp.float32),
             pltpu.VMEM((tokens, span), jnp.bfloat16),
             pltpu.VMEM((N, 2 * rank // N, tokens), jnp.float32),
             pltpu.VMEM((N, 2 * rank // N, tokens), jnp.float32),

time: 60.7 us -> 52.4 us (0.86)
  Pallas kernels: 58.4 us -> 50.3 us
    pallas_call x1, Pallas kernels: 58.4 us -> 50.3 us  [by_kernel(): pl.pallas_call(fused, out_shape=jax.ShapeDtypeStruct((tokens, columns), j...]
where the time goes in v2:
time: 52.4 us; the launch traced here: 52 us
  Pallas kernels  50.3 us (96%)
  local copies, waits for them, and re-layouts  1.67 us (3%)
    pallas_call x1, Pallas kernels, by_kernel(): pl.pallas_call(fused, out_shape=jax.ShapeDtypeStruct((tokens, columns), j...  50.3 us
    unnamed x1, local copies, waits for them, and re-layouts  1.67 us

profile of v2, /device:TPU:0, one launch (start us, length us, event | category | flops | bytes accessed | tf_op | source)
XLA Modules:
  0.0 52.0 jit_solution(10707167784703968128)
XLA Ops:
  0.0 50.3 %shard_map.73 = bf16[256,512]{1,0:T(8,128)(2,1)} custom-call(bf16[16,8192]{1,0:T(8,128)(2,1)} %x_ref.1, bf16[8192,512]{1,0:T(8,128)(2,1)} %w_ref.1, bf16[16384,512]{1,0:T(8,128)(2,1)} %bitcast.6, bf16[16384,512]{1,0:T(8,128)(2,1)} %bitcast.7, s32[2,256]{1,0:T(2,128)} %bitcast.8, f32[2,256]{1,0:T(2,128)} %bitcast.9, s32[256]{0:T(256)} %index_ref.1), custom_call_target="tpu_custom_call" | custom-call | flops 10737418240 | bytes 41943040 | tf_op jit(solution)/shard_map/pallas_call | solution.py:252
  50.3 1.7 %copy.9 = bf16[256,512]{1,0:T(8,128)(2,1)} copy(bf16[256,512]{1,0:T(8,128)(2,1)} %shard_map.73) | data formatting | bytes 524288

commit v3 on v2

--- a/solution.py
+++ b/solution.py
@@ -153,9 +153,12 @@
         pltpu.make_async_copy(
             w_ref.at[pl.ds(q * kq, kq)], w_vm.at[pl.ds(q * kq, kq)], w_sem.at[q]).start()
     each = 2 * rank // N
+    half = tokens // 2
     for k in range(2):
         for j in range(N // 2):
-            partial[k * (N // 2) + j] = carry[k][j * each:(j + 1) * each]
+            part = carry[k][j * each:(j + 1) * each]
+            partial[k * (N // 2) + j] = jnp.concatenate(
+                [part[:, :half], part[:, half:]], axis=0).astype(jnp.bfloat16)
     pieces[0] = partial[me]
     for d in range(1, N):
         to = (me + d) % N
@@ -168,11 +171,10 @@
         pltpu.make_async_remote_copy(
             src_ref=pieces.at[d], dst_ref=pieces.at[d], send_sem=rs_send.at[d], recv_sem=rs_recv.at[d],
             device_id={"tensor": (me + N - d) % N}, device_id_type=MESH).wait_recv()
-    mine = pieces[0]
-    for d in range(1, N):
-        mine = mine + pieces[d]
-    half = tokens // 2
-    reduced[me] = jnp.concatenate([mine[:, :half], mine[:, half:]], axis=0).astype(jnp.bfloat16)
+    mine = pieces[0].astype(jnp.float32)
+    for d in range(1, N):
+        mine = mine + pieces[d].astype(jnp.float32)
+    reduced[me] = mine.astype(jnp.bfloat16)
     for d in range(1, N):
         to = (me + d) % N
         send(reduced.at[me], reduced.at[me], ag_send.at[d], ag_recv.at[d], to)
@@ -261,8 +263,8 @@
             pltpu.VMEM((stored * rank, feat), jnp.bfloat16),
             pltpu.VMEM((stored * rank, columns), jnp.bfloat16),
             pltpu.VMEM((tokens, span), jnp.bfloat16),
-            pltpu.VMEM((N, 2 * rank // N, tokens), jnp.float32),
-            pltpu.VMEM((N, 2 * rank // N, tokens), jnp.float32),
+            pltpu.VMEM((N, 4 * rank // N, tokens // 2), jnp.bfloat16),
+            pltpu.VMEM((N, 4 * rank // N, tokens // 2), jnp.bfloat16),
             pltpu.VMEM((N, 4 * rank // N, tokens // 2), jnp.bfloat16),
             pltpu.VMEM((tokens, columns), jnp.float32),
             dma((2, LOADS)), dma((Q,)), dma((Q + 1,)), dma((N,)), dma((N,)),

time: 52.4 us -> 51.3 us (0.979)
  Pallas kernels: 50.3 us -> 49.3 us
    pallas_call x1, Pallas kernels: 50.3 us -> 49.3 us  [by_kernel(): pl.pallas_call(fused, out_shape=jax.ShapeDtypeStruct((tokens, columns), j...]
where the time goes in v3:
time: 51.3 us; the launch traced here: 51 us
  Pallas kernels  49.3 us (96%)
  local copies, waits for them, and re-layouts  1.67 us (3%)
    pallas_call x1, Pallas kernels, by_kernel(): pl.pallas_call(fused, out_shape=jax.ShapeDtypeStruct((tokens, columns), j...  49.3 us
    unnamed x1, local copies, waits for them, and re-layouts  1.67 us

profile of v3, /device:TPU:0, one launch (start us, length us, event | category | flops | bytes accessed | tf_op | source)
XLA Modules:
  0.0 51.0 jit_solution(7178385953919676859)
XLA Ops:
  0.0 49.3 %shard_map.73 = bf16[256,512]{1,0:T(8,128)(2,1)} custom-call(bf16[16,8192]{1,0:T(8,128)(2,1)} %x_ref.1, bf16[8192,512]{1,0:T(8,128)(2,1)} %w_ref.1, bf16[16384,512]{1,0:T(8,128)(2,1)} %bitcast.6, bf16[16384,512]{1,0:T(8,128)(2,1)} %bitcast.7, s32[2,256]{1,0:T(2,128)} %bitcast.8, f32[2,256]{1,0:T(2,128)} %bitcast.9, s32[256]{0:T(256)} %index_ref.1), custom_call_target="tpu_custom_call" | custom-call | flops 10737418240 | bytes 41943040 | tf_op jit(solution)/shard_map/pallas_call | solution.py:254
  49.3 1.7 %copy.9 = bf16[256,512]{1,0:T(8,128)(2,1)} copy(bf16[256,512]{1,0:T(8,128)(2,1)} %shard_map.73) | data formatting | bytes 524288
